TPU v7x, 32 devices: a whole 2x2x4 slice. The times are simulated.
32 devices in a mesh: query: 4 (over x, core), bank: 8 (over z, y).
Axes of the slice: x: 2, y: 2, z: 4, core: 2. Of those that a mesh axis runs over, the one named last changes fastest.
Arguments:
- queries: bfloat16 [256, 32, 128], P(('query', 'bank'))
- passages: bfloat16 [2048, 128, 128], P('bank')
- passage_home: int32 [2048], replicated, may hold values from 0 to 2047, as said below
- candidates: int32 [256, 16], P(('query', 'bank')), may hold values from 0 to 2047, as said below
- positive: int32 [256], P(('query', 'bank')), may hold values from 0 to 15
Outputs:
- losses: float32 [256], P(('query', 'bank'))
- query_grads: float32 [256, 32, 128], P(('query', 'bank'))
Inputs may be any that keep to these rules, and one draw needn't show every extreme that they name: `passage_home`: each passage id has its own storage row; storage row r lies on bank index r // 256. `candidates`: among the 128 list entries of one device's queries (aligned blocks of 8 queries, in order), at most 48 name passages stored on one bank index; in every block some bank index gets exactly 48, and in each group of 8 consecutive blocks it is the same bank index for all of them.
All inputs are finite; a program needn't handle non-finite values.
Results may differ from a plain program's by a relative error of at most 0.0049.
Values may be sent and summed in bfloat16 or wider, within the bound.
A program may use at most 128 MiB of HBM per device.

v0:
```python
import jax
import jax.numpy as jnp
from jax import lax
from jax.sharding import PartitionSpec as P


def soft_terms(scores):
    largest = jnp.max(scores, axis=-1, keepdims=True)
    raised = jnp.exp(scores - largest)
    totals = jnp.sum(raised, axis=-1, keepdims=True)
    maxima = largest[..., 0] + jnp.log(totals[..., 0])
    weights = (raised / totals).astype(jnp.bfloat16)
    return (maxima, weights)


def contrast(maxima, positive):
    similarity = jnp.sum(maxima, axis=2)
    largest = jnp.max(similarity, axis=1, keepdims=True)
    raised = jnp.exp(similarity - largest)
    totals = jnp.sum(raised, axis=1, keepdims=True)
    picked = jnp.arange(similarity.shape[1], dtype=jnp.int32)[None, :] == positive[:, None]
    losses = (
        largest[:, 0] + jnp.log(totals[:, 0]) - jnp.sum(jnp.where(picked, similarity, 0.0), axis=1)
    )
    coefficients = (raised / totals - picked.astype(jnp.float32)).astype(jnp.bfloat16)
    return (losses, coefficients)


def body(queries, passages, passage_home, candidates, positive):
    shards = lax.axis_size("bank")
    query_rows, query_len, feature_dim = queries.shape
    listed = candidates.shape[1]
    holdings = passages.shape[0]
    tile_len = passages.shape[1]
    entries = query_rows * listed
    capacity = 3 * entries // shards
    storage = passage_home[candidates].reshape(entries)
    owner_bank = storage // holdings
    local_slot = storage % holdings
    member = (owner_bank[:, None] == jnp.arange(shards, dtype=jnp.int32)[None, :]).astype(jnp.int32)
    position = jnp.sum((jnp.cumsum(member, axis=0) - member) * member, axis=1)
    target = owner_bank * capacity + position
    slot_table = (
        jnp.zeros((shards * capacity,), jnp.int32)
        .at[target]
        .set(local_slot)
        .reshape(shards, capacity)
    )
    requests = lax.all_to_all(slot_table, "bank", split_axis=0, concat_axis=0, tiled=True)
    gathered = passages[requests.reshape(-1)].reshape(
        requests.shape[0], requests.shape[1], tile_len * feature_dim
    )
    fetched = lax.all_to_all(gathered, "bank", split_axis=0, concat_axis=0, tiled=True)
    passage_tiles = fetched.reshape(shards * capacity, tile_len, feature_dim)[target].reshape(
        query_rows, listed, tile_len, feature_dim
    )
    scores = jnp.einsum(
        "qid,qkjd->qkij", queries, passage_tiles, preferred_element_type=jnp.float32
    )
    maxima, weights = soft_terms(scores)
    token_basis = jnp.einsum(
        "qkij,qkjd->qkid", weights, passage_tiles, preferred_element_type=jnp.float32
    ).astype(jnp.bfloat16)
    token_basis = token_basis.reshape(query_rows, listed, query_len * feature_dim)
    losses, coefficients = contrast(maxima, positive)
    gradient = jnp.einsum(
        "qk,qkd->qd", coefficients, token_basis, preferred_element_type=jnp.float32
    )
    return (losses, gradient.reshape(query_rows, query_len, feature_dim))


def solution(mesh):
    return jax.shard_map(
        body,
        mesh=mesh,
        in_specs=(
            P(("query", "bank"), None, None),
            P("bank", None, None),
            P(),
            P(("query", "bank"), None),
            P(("query", "bank")),
        ),
        out_specs=(P(("query", "bank")), P(("query", "bank"), None, None)),
        check_vma=False,
    )
```

profile of v0, /device:TPU:0, one launch (start us, length us, event | category | flops | bytes accessed | tf_op | source)
XLA Modules:
  0.0 359.1 jit_solution(1713146112700736741)
XLA Ops:
  0.6 0.0 copy-start
  0.6 0.7 compare_select_fusion
  1.4 0.1 reshape.173
  1.5 1.6 gather_fusion
  3.1 0.1 fusion.6
  3.2 0.2 reduce_window_sum.11
  3.4 0.2 select_reduce_fusion
  3.6 1.0 scatter_custom_fusion
  4.5 0.1 all_to_all.9
  4.6 13.5 %all_to_all.14 = s32[8,1,48]{2,1,0:T(1,128)S(1)} all-to-all(s32[8,1,48]{2,1,0:T(1,128)S(1)} %all_to_all.9), channel_id=1, replica_groups=mesh['query'=4,'bank'=8] {'bank'}, dimensions={0} | all-to-all | bytes 3072 | tf_op jit(solution)/shard_map/all_to_all | solution.py:49
  18.2 0.5 broadcast.167
  18.7 0.7 reduce.5
  19.4 0.1 reshape.165
  19.5 14.3 %gather_fusion.1 = bf16[384,128,128]{2,1,0:T(8,128)(2,1)} fusion(bf16[256,128,128]{2,1,0:T(8,128)(2,1)} %param.6, s32[1024]{0:T(1024)S(1)} %pad_clamp_fusion.1), kind=kCustom, calls=%fused_computation.1 | custom fusion | bytes 25167360 | tf_op jit(solution)/shard_map/gather | solution.py:50
  33.8 19.3 %reshape.166 = bf16[8,48,16384]{2,1,0:T(8,128)(2,1)} reshape(bf16[384,128,128]{2,1,0:T(8,128)(2,1)} %gather_fusion.1) | data formatting | bytes 25165824 | tf_op jit(solution)/shard_map/reshape | solution.py:50
  53.1 5.3 %all-to-all-start.1 = ((bf16[8,48,16384]{2,1,0:T(8,128)(2,1)}), bf16[8,48,16384]{2,1,0:T(8,128)(2,1)}, u32[]{:S(2)}, u32[]{:S(2)}) async-start(bf16[8,48,16384]{2,1,0:T(8,128)(2,1)} %reshape.166), calls=%async_computation.1 | async-start | bytes 25165824 | tf_op jit(solution)/shard_map/all_to_all | solution.py:53
  58.4 272.2 %all-to-all-done.1 = bf16[8,48,16384]{2,1,0:T(8,128)(2,1)} async-done(((bf16[8,48,16384]{2,1,0:T(8,128)(2,1)}), bf16[8,48,16384]{2,1,0:T(8,128)(2,1)}, u32[]{:S(2)}, u32[]{:S(2)}) %all-to-all-start.1) | async-done | bytes 12582944 | tf_op jit(solution)/shard_map/all_to_all | solution.py:53
  330.6 11.5 %copy.10 = bf16[48,8,128,128]{3,2,1,0:T(8,128)(2,1)} copy(bf16[48,8,128,128]{3,1,2,0:T(8,128)(2,1)} %bitcast.11) | data formatting | bytes 25165824
  342.1 7.6 %gather_fusion.2 = bf16[128,128,128]{2,1,0:T(8,128)(2,1)} fusion(bf16[384,128,128]{2,1,0:T(8,128)(2,1)} %bitcast.51, s32[1024]{0:T(1024)S(1)} %pad_clamp_fusion), kind=kCustom, calls=%fused_computation.2 | custom fusion | bytes 8389120 | tf_op jit(solution)/shard_map/gather | solution.py:54
  349.7 0.0 copy-done
  349.7 0.0 copy-start.1
  349.7 4.0 %bitcast_reduce_fusion = (f32[8,16,32]{2,1,0:T(8,128)S(1)}, f32[8,16,128,32]{2,3,1,0:T(8,128)S(1)}) fusion(bf16[8,16,128,128]{3,2,1,0:T(8,128)(2,1)} %bitcast.52, bf16[8,32,128]{2,1,0:T(8,128)(2,1)S(1)} %copy-done), kind=kOutput, calls=%fused_computation.5 | convolution fusion | flops 134737920 | bytes 6373376 | tf_op jit(solution)/shard_map/qid,qkjd->qkij/dot_general | solution.py:57
  353.7 1.3 fusion.1
  355.0 0.1 add_reduce_fusion
  355.1 0.0 copy-done.1
  355.1 0.0 copy-start.2
  355.1 1.5 convolution_convert_fusion
  356.6 0.1 reduce_max.19
  356.8 0.0 copy-done.2
  356.8 0.2 fusion.9
  357.0 0.1 fusion.10
  357.1 0.5 reshape.169
  357.6 0.3 fusion.7
  357.8 0.1 copy.17
  357.9 0.7 copy.16
  358.6 0.5 add_subtract_fusion
  (6 shorter events, 0.1 us)
Async XLA Ops:
  0.6 349.1 %copy-start = (bf16[8,32,128]{2,1,0:T(8,128)(2,1)S(1)}, bf16[8,32,128]{2,1,0:T(8,128)(2,1)}, u32[]{:S(2)}) copy-start(bf16[8,32,128]{2,1,0:T(8,128)(2,1)} %param.5) | copy-start | bytes 196612
  53.1 277.6 %all-to-all-start.1 = ((bf16[8,48,16384]{2,1,0:T(8,128)(2,1)}), bf16[8,48,16384]{2,1,0:T(8,128)(2,1)}, u32[]{:S(2)}, u32[]{:S(2)}) async-start(bf16[8,48,16384]{2,1,0:T(8,128)(2,1)} %reshape.166), calls=%async_computation.1 | async-start | bytes 25165824 | tf_op jit(solution)/shard_map/all_to_all | solution.py:53
  349.7 5.4 %copy-start.1 = (bf16[128,128,128]{2,1,0:T(8,128)(2,1)S(1)}, bf16[128,128,128]{2,1,0:T(8,128)(2,1)}, u32[]{:S(2)}) copy-start(bf16[128,128,128]{2,1,0:T(8,128)(2,1)} %gather_fusion.2) | copy-start | bytes 12582916
  355.1 1.6 copy-start.2
where the time goes:
time: 360 us; the launch traced here: 359 us
  waiting for transfers between devices  272 us (76%)
  local copies, waits for them, and re-layouts  57.3 us (16%)
  blocking collectives  13.5 us (4%)
  matrix products  5.75 us (2%)
  starting transfers between devices  5.34 us (1%)
  other arithmetic  4.22 us (1%)
    all_to_all x1, waiting for transfers between devices, body(): lax.all_to_all(gathered, 'bank', split_axis=0, concat_axis=0, tiled=True)  272 us
    reshape x1, local copies, waits for them, and re-layouts, body(): passages[requests.reshape(-1)]  19.3 us
    gather x1, local copies, waits for them, and re-layouts, body(): passages[requests.reshape(-1)]  14.3 us
    all_to_all x1, blocking collectives, body(): lax.all_to_all(slot_table, 'bank', split_axis=0, concat_axis=0, tiled=True)  13.5 us
    unnamed x8, local copies, waits for them, and re-layouts  12.2 us
    gather x1, local copies, waits for them, and re-layouts, body(): fetched.reshape(shards * capacity, tile_len, feature_dim)[target]  7.58 us
  transfers between devices with their start and end apart: 1, of which 1 were waited for; matrix products, arithmetic and copies ran while one was open for 0% of the time, Pallas kernels for 0%

commit v1 on v0

v1 whole, which is shorter than its diff:
```python
import jax
import jax.numpy as jnp
from jax import lax
from jax.experimental import pallas as pl
from jax.experimental.pallas import tpu as pltpu
from jax.sharding import PartitionSpec as P

GROUP = 8


def pair_kernel(row_ref, qid_ref, queries_ref, passages_ref, basis_ref, sim_ref):
    slots = row_ref.shape[0]

    @pl.loop(0, slots // GROUP)
    def _(group):
        first = group * GROUP
        tiles = [passages_ref[row_ref[first + u]] for u in range(GROUP)]
        scores = [
            lax.dot_general(
                queries_ref[qid_ref[first + u]],
                tiles[u],
                (((1,), (1,)), ((), ())),
                preferred_element_type=jnp.float32,
            )
            for u in range(GROUP)
        ]
        largest = [jnp.max(s, axis=1, keepdims=True) for s in scores]
        raised = [jnp.exp(s - m) for s, m in zip(scores, largest)]
        totals = [jnp.sum(r, axis=1, keepdims=True) for r in raised]
        weights = [(r / t).astype(jnp.bfloat16) for r, t in zip(raised, totals)]
        for u in range(GROUP):
            basis_ref[first + u] = jnp.dot(
                weights[u], tiles[u], preferred_element_type=jnp.float32
            ).astype(jnp.bfloat16)
        rows = [
            jnp.sum(m + jnp.log(t), axis=0, keepdims=True) for m, t in zip(largest, totals)
        ]
        sim_ref[pl.ds(pl.multiple_of(first, GROUP), GROUP), :] = jnp.broadcast_to(
            jnp.concatenate(rows, axis=0), (GROUP, sim_ref.shape[1])
        )


def pair_terms(rows, qids, queries, passages):
    slots = rows.shape[0]
    query_len, feature_dim = queries.shape[1:]
    return pl.pallas_call(
        pair_kernel,
        out_shape=(
            jax.ShapeDtypeStruct((slots, query_len, feature_dim), jnp.bfloat16),
            jax.ShapeDtypeStruct((slots, 128), jnp.float32),
        ),
        in_specs=[pl.BlockSpec(memory_space=pltpu.SMEM)] * 2
        + [pl.BlockSpec(memory_space=pltpu.VMEM)] * 2,
        out_specs=(pl.BlockSpec(memory_space=pltpu.VMEM),) * 2,
        compiler_params=pltpu.CompilerParams(vmem_limit_bytes=40 * 1024 * 1024),
    )(rows, qids, queries, passages)


def slot_list(storage, positive, holdings, capacity):
    count, listed = storage.shape
    me = lax.axis_index("bank")
    owned = (storage // holdings == me).reshape(-1)
    entry = jnp.arange(count * listed, dtype=jnp.int32)
    picked = (jnp.arange(listed, dtype=jnp.int32)[None, :] == positive[:, None]).astype(jnp.int32)
    code = (entry * 2 + picked.reshape(-1)) * holdings + (storage % holdings).reshape(-1)
    position = jnp.cumsum(owned.astype(jnp.int32)) - 1
    target = jnp.where(owned, position, capacity)
    table = jnp.full((capacity,), -1, jnp.int32).at[target].set(code, mode="drop")
    valid = table >= 0
    table = jnp.maximum(table, 0)
    rows = table % holdings
    rest = table // holdings
    return rows, rest // 2 // listed, valid, rest % 2


def body(queries, passages, passage_home, candidates, positive):
    shards = lax.axis_size("bank")
    query_rows, query_len, feature_dim = queries.shape
    listed = candidates.shape[1]
    holdings = passages.shape[0]
    entries = query_rows * listed
    capacity = 3 * entries
    group = shards * query_rows
    info = jnp.concatenate([passage_home[candidates], positive[:, None]], axis=1)
    infos = lax.all_gather(info, "bank", axis=0, tiled=True)
    all_queries = lax.all_gather(queries, "bank", axis=0, tiled=True)
    rows, qids, valid, picked = slot_list(infos[:, :listed], infos[:, listed], holdings, capacity)
    basis, sims = pair_terms(rows, qids, all_queries, passages)
    match = (qids[None, :] == jnp.arange(group, dtype=jnp.int32)[:, None]) & valid[None, :]
    chosen = match & (picked[None, :] > 0)
    table = jnp.where(match, sims[:, 0][None, :], -jnp.inf)
    largest = jnp.max(table, axis=1)
    safe = jnp.where(largest == -jnp.inf, 0.0, largest)
    partial = jnp.sum(jnp.exp(table - safe[:, None]), axis=1)
    wanted = jnp.sum(jnp.where(chosen, table, 0.0), axis=1)
    stats = lax.all_gather(jnp.stack([largest, partial, wanted]), "bank", axis=0, tiled=False)
    top = jnp.max(stats[:, 0], axis=0)
    total = jnp.sum(stats[:, 1] * jnp.exp(stats[:, 0] - top[None, :]), axis=0)
    losses = top + jnp.log(total) - jnp.sum(stats[:, 2], axis=0)
    mine = lax.axis_index("bank") * query_rows
    losses = lax.dynamic_slice_in_dim(losses, mine, query_rows, 0)
    shares = jnp.exp(table - top[:, None]) / total[:, None]
    coefficients = (shares - chosen.astype(jnp.float32)).astype(jnp.bfloat16)
    part = jnp.dot(
        coefficients,
        basis.reshape(capacity, query_len * feature_dim),
        preferred_element_type=jnp.float32,
    ).astype(jnp.bfloat16)
    parts = lax.all_to_all(
        part.reshape(shards, query_rows, query_len * feature_dim), "bank", 0, 0, tiled=True
    )
    gradient = jnp.sum(parts.astype(jnp.float32), axis=0)
    return (losses, gradient.reshape(query_rows, query_len, feature_dim))


def solution(mesh):
    return jax.shard_map(
        body,
        mesh=mesh,
        in_specs=(
            P(("query", "bank"), None, None),
            P("bank", None, None),
            P(),
            P(("query", "bank"), None),
            P(("query", "bank")),
        ),
        out_specs=(P(("query", "bank")), P(("query", "bank"), None, None)),
        check_vma=False,
    )
```

time: 360 us -> 146 us (0.41)
  waiting for transfers between devices: 272 us -> 9.69 us
  blocking collectives: 13.5 us -> 89.4 us
  local copies, waits for them, and re-layouts: 57.3 us -> 11.2 us
  Pallas kernels: 0 us -> 26.4 us
  matrix products: 5.75 us -> 1.98 us
    all_to_all x1, waiting for transfers between devices: 272 us -> 9.69 us  [body(): lax.all_to_all(part.reshape(shards, query_rows, query_len * feature_dim),...]
    all_gather x0 -> x3, blocking collectives: none -> 89.4 us  [the longest x1 32.2 us: body(): infos = lax.all_gather(info, 'bank', axis=0, tiled=True)]
    pallas_call x0 -> x1, Pallas kernels: none -> 26.4 us  [pair_terms(): pl.pallas_call(pair_kernel, out_shape=(jax.ShapeDtypeStruct((slots, query...]
    gather x3 -> x2, local copies, waits for them, and re-layouts: 23.5 us -> 1.23 us  [body(): passage_home[candidates]]
    reshape x3 -> x2, local copies, waits for them, and re-layouts: 19.9 us -> 0.17 us  [the longest x1 0.09 us: slot_list(): owned = (storage // holdings == me).reshape(-1)]
    all_to_all x1 -> x0, blocking collectives: 13.5 us -> none  [body(): lax.all_to_all(slot_table, 'bank', split_axis=0, concat_axis=0, tiled=True)]
    unnamed x8 -> x9, local copies, waits for them, and re-layouts: 12.2 us -> 4.08 us
    dot_general x3 -> x1, matrix products: 5.75 us -> 1.98 us  [body(): jnp.dot(coefficients, basis.reshape(capacity, query_len * feature_dim), p...]
where the time goes in v1:
time: 146 us
  blocking collectives  89.4 us (61%)
  Pallas kernels  26.4 us (18%)
  local copies, waits for them, and re-layouts  11.2 us (8%)
  waiting for transfers between devices  9.69 us (7%)
  starting transfers between devices  4.72 us (3%)
  matrix products  1.98 us (1%)
  other arithmetic  1.86 us (1%)
    all_gather x1, blocking collectives, body(): infos = lax.all_gather(info, 'bank', axis=0, tiled=True)  32.2 us
    all_gather x1, blocking collectives, body(): all_queries = lax.all_gather(queries, 'bank', axis=0, tiled=True)  31.2 us
    pallas_call x1, Pallas kernels, pair_terms(): pl.pallas_call(pair_kernel, out_shape=(jax.ShapeDtypeStruct((slots, query...  26.4 us
    all_gather x1, blocking collectives, body(): lax.all_gather(jnp.stack([largest, partial, wanted]), 'bank', axis=0, til...  26 us
    all_to_all x1, waiting for transfers between devices, body(): lax.all_to_all(part.reshape(shards, query_rows, query_len * feature_dim),...  9.69 us
    all_to_all x1, starting transfers between devices, body(): lax.all_to_all(part.reshape(shards, query_rows, query_len * feature_dim),...  4.72 us
    scatter x1, local copies, waits for them, and re-layouts, slot_list(): jnp.full((capacity,), -1, jnp.int32).at[target].set(code, mode='drop')  4.3 us
    unnamed x9, local copies, waits for them, and re-layouts  4.08 us
  transfers between devices with their start and end apart: 1, of which 1 were waited for; matrix products, arithmetic and copies ran while one was open for 0% of the time, Pallas kernels for 0%

profile of v1, /device:TPU:0, one launch (start us, length us, event | category | flops | bytes accessed | tf_op | source)
XLA Modules:
  0.0 146.0 jit_solution(11764761498854206855)
XLA Ops:
  0.6 0.0 copy-start
  0.6 0.0 copy-start.3
  0.7 0.0 copy-start.2
  0.7 0.7 compare_select_fusion.1
  1.4 0.1 reshape.103
  1.5 0.0 copy-done
  1.5 1.1 gather_fusion
  2.6 0.1 reshape.102
  2.7 0.0 copy-done.3
  2.7 0.1 copy.13
  2.8 0.1 pad_add_fusion
  2.9 32.2 %all_gather.12 = s32[64,17]{1,0:T(8,128)S(1)} all-gather(s32[8,17]{1,0:T(8,128)S(1)} %pad_add_fusion), channel_id=1, replica_groups=mesh['query'=4,'bank'=8] {'bank'}, dimensions={0}, use_global_device_ids=true | all-gather | bytes 4896 | tf_op jit(solution)/shard_map/all_gather | solution.py:85
  35.1 0.2 slice_reduce_fusion.1
  35.3 0.1 fusion.22
  35.4 0.1 reshape.100
  35.4 0.1 reshape.95
  35.6 0.1 reshape.99
  35.6 0.3 reduce-window.9
  35.9 0.1 slice.27
  36.0 0.1 slice_reduce_fusion.3
  36.1 0.1 add_add_fusion
  36.2 0.1 reshape.93
  36.3 4.3 %scatter_custom_fusion = s32[384]{0:T(512)S(1)} fusion(s32[1024]{0:T(1024)S(1)} %bitcast.30, s32[1024]{0:T(1024)S(1)} %multiply_add_fusion, s32[]{:T(128)} %constant.92.clone.1), kind=kCustom, calls=%fused_computation.76 | custom fusion | bytes 1540 | tf_op jit(solution)/shard_map/scatter | solution.py:68
  40.7 0.0 copy-done.2
  40.7 31.2 %all_gather.13.queries_ref = bf16[64,32,128]{2,1,0:T(8,128)(2,1)S(1)} all-gather(bf16[8,32,128]{2,1,0:T(8,128)(2,1)S(1)} %copy-done.2), channel_id=1, replica_groups=mesh['query'=4,'bank'=8] {'bank'}, dimensions={0}, use_global_device_ids=true | all-gather | bytes 589824 | tf_op jit(solution)/shard_map/all_gather | solution.py:86
  71.9 0.0 copy-start.1
  71.9 3.4 %copy-done.1 = bf16[256,128,128]{2,1,0:T(8,128)(2,1)S(1)} copy-done((bf16[256,128,128]{2,1,0:T(8,128)(2,1)S(1)}, bf16[256,128,128]{2,1,0:T(8,128)(2,1)}, u32[]{:S(2)}) %copy-start.1) | copy-done | bytes 8388632
  75.3 26.4 %shard_map.68 = (bf16[384,32,128]{2,1,0:T(8,128)(2,1)S(1)}, f32[384,128]{1,0:T(8,128)S(1)}) custom-call(s32[384]{0:T(512)S(1)} %get-tuple-element.18.row_ref, s32[384]{0:T(512)S(1)} %get-tuple-element.17.qid_ref, bf16[64,32,128]{2,1,0:T(8,128)(2,1)S(1)} %all_gather.13.queries_ref, bf16[256,128,128]{2,1,0:T(8,128)(2,1)S(1)} %copy-done.1), custom_call_target="tpu_custom_call" | custom-call | tf_op jit(solution)/shard_map/pallas_call | solution.py:46
  101.7 0.2 slice_reduce_fusion
  101.8 0.1 select_reduce_fusion
  102.0 0.2 fusion.4
  102.2 26.0 %all-gather.1 = f32[8,3,64]{2,1,0:T(4,128)S(1)} all-gather(f32[1,3,64]{2,1,0:T(4,128)S(1)} %maximum_bitcast_fusion), channel_id=2, replica_groups=mesh['query'=4,'bank'=8] {'bank'}, dimensions={0}, use_global_device_ids=true | all-gather | bytes 6912 | tf_op jit(solution)/shard_map/all_gather | solution.py:96
  128.3 2.0 %fusion = bf16[8,8,4096]{2,1,0:T(8,128)(2,1)} fusion(bf16[48,8,32,128]{3,2,1,0:T(8,128)(2,1)S(1)} %bitcast.23, f32[64]{0:T(128)S(1)} %multiply_reduce_fusion, f32[64]{0:T(128)S(1)} %reduce_max.19, f32[384]{0:T(512)S(1)} %slice_reduce_fusion, s32[384]{0:T(512)S(1)} %get-tuple-element.17.qid_ref, pred[384]{0:T(512)(128)(4,1)S(1)} %get-tuple-element.15, ...), kind=kOutput, calls=%fused_computation.3 | convolution fusion | flops 201809920 | bytes 3674368 | tf_op jit(solution)/shard_map/dot_general | solution.py:104
  130.3 4.7 %all-to-all-start = ((bf16[8,8,4096]{2,1,0:T(8,128)(2,1)}), bf16[8,8,4096]{2,1,0:T(8,128)(2,1)S(1)}, u32[]{:S(2)}, u32[]{:S(2)}) async-start(bf16[8,8,4096]{2,1,0:T(8,128)(2,1)} %fusion), calls=%async_computation | async-start | bytes 1048576 | tf_op jit(solution)/shard_map/all_to_all | solution.py:109
  135.0 0.6 dynamic_slice.3
  135.6 9.7 %all-to-all-done = bf16[8,8,4096]{2,1,0:T(8,128)(2,1)S(1)} async-done(((bf16[8,8,4096]{2,1,0:T(8,128)(2,1)}), bf16[8,8,4096]{2,1,0:T(8,128)(2,1)S(1)}, u32[]{:S(2)}, u32[]{:S(2)}) %all-to-all-start) | async-done | bytes 524320 | tf_op jit(solution)/shard_map/all_to_all | solution.py:109
  145.3 0.1 convert_reduce_fusion
  145.3 0.7 copy.23
  (14 shorter events, 0.2 us)
Async XLA Ops:
  0.6 0.9 copy-start
  0.6 2.1 %copy-start.3 = (s32[8]{0:T(128)S(1)}, s32[8]{0:T(128)}, u32[]{:S(2)}) copy-start(s32[8]{0:T(128)} %param.9) | copy-start | bytes 100
  0.7 40.0 %copy-start.2 = (bf16[8,32,128]{2,1,0:T(8,128)(2,1)S(1)}, bf16[8,32,128]{2,1,0:T(8,128)(2,1)}, u32[]{:S(2)}) copy-start(bf16[8,32,128]{2,1,0:T(8,128)(2,1)} %param.5) | copy-start | bytes 196612
  71.9 3.4 %copy-start.1 = (bf16[256,128,128]{2,1,0:T(8,128)(2,1)S(1)}, bf16[256,128,128]{2,1,0:T(8,128)(2,1)}, u32[]{:S(2)}) copy-start(bf16[256,128,128]{2,1,0:T(8,128)(2,1)} %passages_ref.1) | copy-start | bytes 25165828
  130.3 15.0 %all-to-all-start = ((bf16[8,8,4096]{2,1,0:T(8,128)(2,1)}), bf16[8,8,4096]{2,1,0:T(8,128)(2,1)S(1)}, u32[]{:S(2)}, u32[]{:S(2)}) async-start(bf16[8,8,4096]{2,1,0:T(8,128)(2,1)} %fusion), calls=%async_computation | async-start | bytes 1048576 | tf_op jit(solution)/shard_map/all_to_all | solution.py:109

commit v2 on v1

v2 whole, which is shorter than its diff:
```python
import functools

import jax
import jax.numpy as jnp
from jax import lax
from jax.experimental import pallas as pl
from jax.experimental.pallas import tpu as pltpu
from jax.sharding import PartitionSpec as P

GROUP = 8


MESH = pl.DeviceIdType.MESH


def quarter_sum(x):
    n = x.shape[0] // 4
    return (x[:n] + x[n : 2 * n]) + (x[2 * n : 3 * n] + x[3 * n :])


def quarter_product(x):
    n = x.shape[0] // 4
    return (x[:n] * x[n : 2 * n]) * (x[2 * n : 3 * n] * x[3 * n :])


def pair_kernel(row_ref, qid_ref, queries_ref, passages_ref, basis_ref, sim_ref):
    slots = row_ref.shape[0]

    @pl.loop(0, slots // GROUP)
    def _(group):
        first = group * GROUP
        tiles = [passages_ref[row_ref[first + u]] for u in range(GROUP)]
        scores = [
            lax.dot_general(
                queries_ref[qid_ref[first + u]],
                tiles[u],
                (((1,), (1,)), ((), ())),
                preferred_element_type=jnp.float32,
            )
            for u in range(GROUP)
        ]
        largest = [jnp.max(s, axis=1, keepdims=True) for s in scores]
        raised = [jnp.exp(s - m) for s, m in zip(scores, largest)]
        totals = [jnp.sum(r, axis=1, keepdims=True) for r in raised]
        guesses = [pl.reciprocal(t, approx=True) for t in totals]
        inverse = [g * (2.0 - t * g) for g, t in zip(guesses, totals)]
        weights = [(r * v).astype(jnp.bfloat16) for r, v in zip(raised, inverse)]
        for u in range(GROUP):
            basis_ref[first + u] = jnp.dot(
                weights[u], tiles[u], preferred_element_type=jnp.float32
            ).astype(jnp.bfloat16)
        rows = [
            jnp.sum(quarter_sum(m) + jnp.log(quarter_product(t)), axis=0, keepdims=True)
            for m, t in zip(largest, totals)
        ]
        sim_ref[pl.ds(pl.multiple_of(first, GROUP), GROUP), :] = jnp.broadcast_to(
            jnp.concatenate(rows, axis=0), (GROUP, sim_ref.shape[1])
        )


def pair_terms(rows, qids, queries, passages):
    slots = rows.shape[0]
    query_len, feature_dim = queries.shape[1:]
    return pl.pallas_call(
        pair_kernel,
        out_shape=(
            jax.ShapeDtypeStruct((slots, query_len, feature_dim), jnp.bfloat16),
            jax.ShapeDtypeStruct((slots, 128), jnp.float32),
        ),
        in_specs=[pl.BlockSpec(memory_space=pltpu.SMEM)] * 2
        + [pl.BlockSpec(memory_space=pltpu.VMEM)] * 2,
        out_specs=(pl.BlockSpec(memory_space=pltpu.VMEM),) * 2,
        compiler_params=pltpu.CompilerParams(vmem_limit_bytes=40 * 1024 * 1024),
    )(rows, qids, queries, passages)


def greet(shards, me):
    barrier = pltpu.get_barrier_semaphore()
    for step in range(1, shards):
        pl.semaphore_signal(
            barrier, inc=1, device_id={"bank": lax.rem(me + step, shards)}, device_id_type=MESH
        )
    pl.semaphore_wait(barrier, shards - 1)


def gather_kernel(shards, inner, q_ref, info_ref, all_q_ref, all_info_ref, sends, recvs, isends, irecvs):
    outer = shards // inner
    me = lax.axis_index("bank")
    z, y = me // inner, lax.rem(me, inner)
    rows = q_ref.shape[0]

    def place(index):
        return pl.ds(pl.multiple_of(index * rows, rows), rows)

    def peer(dz, dy):
        return lax.rem(z + dz, outer) * inner + lax.rem(y + dy, inner)

    def send(src, block, slot, target):
        copy = pltpu.make_async_remote_copy(
            src_ref=src,
            dst_ref=all_q_ref.at[place(block)],
            send_sem=sends.at[slot],
            recv_sem=recvs.at[slot],
            device_id={"bank": target},
            device_id_type=MESH,
        )
        copy.start()
        return copy

    greet(shards, me)
    copies = {}
    for dz in range(1, outer):
        copies[dz * inner] = send(q_ref, me, dz * inner, peer(dz, 0))
    small = []
    for step in range(1, shards):
        copy = pltpu.make_async_remote_copy(
            src_ref=info_ref,
            dst_ref=all_info_ref.at[place(me)],
            send_sem=isends.at[step],
            recv_sem=irecvs.at[step],
            device_id={"bank": lax.rem(me + step, shards)},
            device_id_type=MESH,
        )
        copy.start()
        small.append(copy)
    for dy in range(1, inner):
        copies[dy] = send(q_ref, me, dy, peer(0, dy))
    all_q_ref[place(me)] = q_ref[...]
    all_info_ref[place(me)] = info_ref[...]
    for dz in range(1, outer):
        copies[dz * inner].wait_recv()
        source = lax.rem(z + outer - dz, outer) * inner + y
        for dy in range(1, inner):
            copies[dz * inner + dy] = send(
                all_q_ref.at[place(source)], source, dz * inner + dy, peer(0, dy)
            )
    for slot, copy in copies.items():
        if slot < inner or slot % inner:
            copy.wait_recv()
        copy.wait_send()
    for copy in small:
        copy.wait()


def gather_queries(queries, info):
    shards = lax.axis_size("bank")
    inner = 1
    while (2 * inner) ** 2 <= shards:
        inner *= 2
    vmem = pl.BlockSpec(memory_space=pltpu.VMEM)
    return pl.pallas_call(
        functools.partial(gather_kernel, shards, inner),
        out_shape=(
            jax.ShapeDtypeStruct((shards * queries.shape[0],) + queries.shape[1:], queries.dtype),
            jax.ShapeDtypeStruct((shards * info.shape[0], info.shape[1]), info.dtype),
        ),
        in_specs=[vmem, vmem],
        out_specs=(vmem, vmem),
        scratch_shapes=[pltpu.SemaphoreType.DMA((shards,))] * 4,
        compiler_params=pltpu.CompilerParams(
            collective_id=0, has_side_effects=True, vmem_limit_bytes=16 * 1024 * 1024
        ),
    )(queries, info)


def contrast_kernel(shards, sim_ref, meta_ref, coef_ref, loss_ref, slots, sends, recvs):
    me = lax.axis_index("bank")
    width = coef_ref.shape[1]
    capacity = sim_ref.shape[0]
    meta = meta_ref[...]
    lane = lax.broadcasted_iota(jnp.int32, (capacity, width), 1)
    chosen = meta == lane * 2 + 1
    match = chosen | (meta == lane * 2)
    table = jnp.where(match, sim_ref[:, :1], -jnp.inf)
    largest = jnp.max(table, axis=0, keepdims=True)
    safe = jnp.where(largest == -jnp.inf, 0.0, largest)
    partial = jnp.sum(jnp.exp(table - safe), axis=0, keepdims=True)
    wanted = jnp.sum(jnp.where(chosen, table, 0.0), axis=0, keepdims=True)
    slots[me] = jnp.concatenate([largest, partial, wanted, jnp.zeros((5, width), jnp.float32)], axis=0)
    greet(shards, me)
    copies = []
    for step in range(1, shards):
        copy = pltpu.make_async_remote_copy(
            src_ref=slots.at[me],
            dst_ref=slots.at[me],
            send_sem=sends.at[step],
            recv_sem=recvs.at[step],
            device_id={"bank": lax.rem(me + step, shards)},
            device_id_type=MESH,
        )
        copy.start()
        copies.append(copy)
    for copy in copies:
        copy.wait()
    tops = [slots[b, 0:1, :] for b in range(shards)]
    top = functools.reduce(jnp.maximum, tops)
    top = jnp.where(top == -jnp.inf, 0.0, top)
    total = sum(slots[b, 1:2, :] * jnp.exp(tops[b] - top) for b in range(shards))
    picked = sum(slots[b, 2:3, :] for b in range(shards))
    loss_ref[...] = jnp.broadcast_to(top + jnp.log(total) - picked, loss_ref.shape)
    total = jnp.where(total == 0.0, 1.0, total)
    shares = jnp.exp(table - top) / total
    coef_ref[...] = (shares - jnp.where(chosen, 1.0, 0.0)).astype(coef_ref.dtype)


def contrast(sims, meta, group):
    shards = lax.axis_size("bank")
    width = -(-group // 128) * 128
    vmem = pl.BlockSpec(memory_space=pltpu.VMEM)
    return pl.pallas_call(
        functools.partial(contrast_kernel, shards),
        out_shape=(
            jax.ShapeDtypeStruct((sims.shape[0], width), jnp.bfloat16),
            jax.ShapeDtypeStruct((8, width), jnp.float32),
        ),
        in_specs=[vmem, vmem],
        out_specs=(vmem, vmem),
        scratch_shapes=[
            pltpu.VMEM((shards, 8, width), jnp.float32),
            pltpu.SemaphoreType.DMA((shards,)),
            pltpu.SemaphoreType.DMA((shards,)),
        ],
        compiler_params=pltpu.CompilerParams(
            collective_id=1, has_side_effects=True, vmem_limit_bytes=16 * 1024 * 1024
        ),
    )(sims, meta)


def slot_list(storage, positive, holdings, capacity):
    count, listed = storage.shape
    me = lax.axis_index("bank")
    owned = (storage // holdings == me).reshape(-1)
    entry = jnp.arange(count * listed, dtype=jnp.int32)
    picked = (jnp.arange(listed, dtype=jnp.int32)[None, :] == positive[:, None]).astype(jnp.int32)
    query = entry // listed
    code = (query * 2 + picked.reshape(-1)) * holdings + (storage % holdings).reshape(-1)
    position = jnp.cumsum(owned.astype(jnp.int32)) - 1
    target = jnp.where(owned, position, -1)
    here = target[None, :] == jnp.arange(capacity, dtype=jnp.int32)[:, None]
    table = jnp.sum(jnp.where(here, code[None, :] + 1, 0), axis=1) - 1
    meta = jnp.where(table >= 0, table // holdings, -1)
    table = jnp.maximum(table, 0)
    return table % holdings, table // holdings // 2, meta


def body(queries, passages, passage_home, candidates, positive):
    shards = lax.axis_size("bank")
    query_rows, query_len, feature_dim = queries.shape
    listed = candidates.shape[1]
    holdings = passages.shape[0]
    capacity = 3 * query_rows * listed
    group = shards * query_rows
    info = jnp.concatenate([passage_home[candidates], positive[:, None]], axis=1)
    info = jnp.pad(info, ((0, 0), (0, 128 - info.shape[1])))
    all_queries, infos = gather_queries(queries, info)
    rows, qids, meta = slot_list(infos[:, :listed], infos[:, listed], holdings, capacity)
    basis, sims = pair_terms(rows, qids, all_queries, passages)
    coefficients, losses = contrast(sims, meta[:, None], group)
    mine = lax.axis_index("bank") * query_rows
    losses = lax.dynamic_slice_in_dim(losses[0], mine, query_rows, 0)
    part = lax.dot_general(
        coefficients[:, :group],
        basis.reshape(capacity, query_len * feature_dim),
        (((0,), (0,)), ((), ())),
        preferred_element_type=jnp.float32,
    ).astype(jnp.bfloat16)
    parts = lax.all_to_all(
        part.reshape(shards, query_rows, query_len * feature_dim), "bank", 0, 0, tiled=True
    )
    gradient = jnp.sum(parts.astype(jnp.float32), axis=0)
    return (losses, gradient.reshape(query_rows, query_len, feature_dim))


def solution(mesh):
    return jax.shard_map(
        body,
        mesh=mesh,
        in_specs=(
            P(("query", "bank"), None, None),
            P("bank", None, None),
            P(),
            P(("query", "bank"), None),
            P(("query", "bank")),
        ),
        out_specs=(P(("query", "bank")), P(("query", "bank"), None, None)),
        check_vma=False,
    )
```

time: 146 us -> 77 us (0.53)
  blocking collectives: 89.4 us -> 0 us
  Pallas kernels: 26.4 us -> 49.6 us
  local copies, waits for them, and re-layouts: 11.2 us -> 6.74 us
    all_gather x3 -> x0, blocking collectives: 89.4 us -> none  [the longest x1 32.2 us: body(): infos = lax.all_gather(info, 'bank', axis=0, tiled=True)]
    pallas_call x0 -> x2, Pallas kernels: none -> 23 us  [the longest x1 15.9 us: gather_queries(): pl.pallas_call(functools.partial(gather_kernel, shards, inner), out_shape...]
    scatter x1 -> x0, local copies, waits for them, and re-layouts: 4.3 us -> none  [slot_list(): jnp.full((capacity,), -1, jnp.int32).at[target].set(code, mode='drop')]
  transfers between devices with their start and end apart: 1 -> 1, of which waited for: 1 -> 1; matrix products, arithmetic and copies ran while one was open for 0% -> 1% of each run, Pallas kernels for 0% -> 0%
where the time goes in v2:
time: 77 us; the launch traced here: 76.7 us
  Pallas kernels  49.6 us (64%)
  waiting for transfers between devices  10.4 us (14%)
  local copies, waits for them, and re-layouts  6.74 us (9%)
  starting transfers between devices  5.45 us (7%)
  matrix products  1.94 us (3%)
  other arithmetic  1.84 us (2%)
    pallas_call x1, Pallas kernels, pair_terms(): pl.pallas_call(pair_kernel, out_shape=(jax.ShapeDtypeStruct((slots, query...  26.6 us
    pallas_call x1, Pallas kernels, gather_queries(): pl.pallas_call(functools.partial(gather_kernel, shards, inner), out_shape...  15.9 us
    all_to_all x1, waiting for transfers between devices, body(): lax.all_to_all(part.reshape(shards, query_rows, query_len * feature_dim),...  10.4 us
    pallas_call x1, Pallas kernels, contrast(): pl.pallas_call(functools.partial(contrast_kernel, shards), out_shape=(jax...  7.08 us
    all_to_all x1, starting transfers between devices, body(): lax.all_to_all(part.reshape(shards, query_rows, query_len * feature_dim),...  5.45 us
    unnamed x9, local copies, waits for them, and re-layouts  4.08 us
    dot_general x1, matrix products, body(): lax.dot_general(coefficients[:, :group], basis.reshape(capacity, query_le...  1.94 us
  transfers between devices with their start and end apart: 1, of which 1 were waited for; matrix products, arithmetic and copies ran while one was open for 1% of the time, Pallas kernels for 0%

profile of v2, /device:TPU:0, one launch (start us, length us, event | category | flops | bytes accessed | tf_op | source)
XLA Modules:
  0.0 76.7 jit_solution(6011421497903888958)
XLA Ops:
  0.6 0.0 copy-start
  0.6 0.0 copy-start.3
  0.7 0.0 copy-start.2
  0.7 0.7 compare_select_fusion
  1.4 0.1 reshape.161
  1.5 0.0 copy-done
  1.5 1.1 %gather_fusion = s32[128]{0:T(128)S(1)} fusion(s32[2048]{0:T(1024)S(1)} %copy-done, s32[1024]{0:T(1024)S(1)} %pad_clamp_fusion), kind=kCustom, calls=%fused_computation | custom fusion | bytes 1536 | tf_op jit(solution)/shard_map/gather | solution.py:253
  2.6 0.1 reshape.160
  2.7 0.0 copy-done.3
  2.7 0.1 copy.14
  2.8 0.1 pad_add_fusion
  2.9 0.0 copy-done.2
  2.9 15.9 %shard_map.68 = (bf16[64,32,128]{2,1,0:T(8,128)(2,1)S(1)}, s32[64,128]{1,0:T(8,128)S(1)}) custom-call(bf16[8,32,128]{2,1,0:T(8,128)(2,1)S(1)} %copy-done.2, s32[8,128]{1,0:T(8,128)S(1)} %pad.4.info_ref), custom_call_target="tpu_custom_call" | custom-call | tf_op jit(solution)/shard_map/pallas_call | solution.py:151
  18.8 0.2 slice_reduce_fusion
  19.1 0.1 reshape.153
  19.2 0.1 reshape.157
  19.2 0.3 reduce-window.9
  19.5 0.1 slice.20
  19.6 0.1 slice_reduce_fusion.1
  19.7 0.1 reshape.151
  19.8 0.1 fusion.14
  19.9 0.1 reshape.158
  20.0 0.1 fusion.20
  20.1 0.2 select_reduce_fusion
  20.3 0.2 fusion.7.meta_ref
  20.5 0.0 copy-start.1
  20.6 3.4 %copy-done.1 = bf16[256,128,128]{2,1,0:T(8,128)(2,1)S(1)} copy-done((bf16[256,128,128]{2,1,0:T(8,128)(2,1)S(1)}, bf16[256,128,128]{2,1,0:T(8,128)(2,1)}, u32[]{:S(2)}) %copy-start.1) | copy-done | bytes 8388632
  23.9 26.6 %shard_map.69 = (bf16[384,32,128]{2,1,0:T(8,128)(2,1)S(1)}, f32[384,128]{1,0:T(8,128)S(1)}) custom-call(s32[384]{0:T(512)S(1)} %get-tuple-element.18.row_ref, s32[384]{0:T(512)S(1)} %get-tuple-element.19.qid_ref, bf16[64,32,128]{2,1,0:T(8,128)(2,1)S(1)} %get-tuple-element.9.queries_ref, bf16[256,128,128]{2,1,0:T(8,128)(2,1)S(1)} %copy-done.1), custom_call_target="tpu_custom_call" | custom-call | tf_op jit(solution)/shard_map/pallas_call | solution.py:64
  50.5 7.1 %shard_map.70 = (bf16[384,128]{1,0:T(8,128)(2,1)S(1)}, f32[8,128]{1,0:T(8,128)S(1)}) custom-call(f32[384,128]{1,0:T(8,128)S(1)} %get-tuple-element.10.sim_ref, s32[384,1]{1,0:T(8,128)S(1)} %fusion.7.meta_ref), custom_call_target="tpu_custom_call" | custom-call | tf_op jit(solution)/shard_map/pallas_call | solution.py:210
  57.6 1.9 %fusion = bf16[8,8,4096]{2,1,0:T(8,128)(2,1)} fusion(bf16[48,8,32,128]{3,2,1,0:T(8,128)(2,1)S(1)} %bitcast.15, bf16[384,128]{1,0:T(8,128)(2,1)S(1)} %get-tuple-element.12), kind=kOutput, calls=%fused_computation.2 | convolution fusion | flops 201588736 | bytes 3768320 | tf_op jit(solution)/shard_map/dot_general | solution.py:261
  59.5 5.5 %all-to-all-start = ((bf16[8,8,4096]{2,1,0:T(8,128)(2,1)}), bf16[8,8,4096]{2,1,0:T(8,128)(2,1)S(1)}, u32[]{:S(2)}, u32[]{:S(2)}) async-start(bf16[8,8,4096]{2,1,0:T(8,128)(2,1)} %fusion), calls=%async_computation | async-start | bytes 1048576 | tf_op jit(solution)/shard_map/all_to_all | solution.py:267
  65.0 0.6 dynamic-slice_bitcast_fusion
  65.6 10.4 %all-to-all-done = bf16[8,8,4096]{2,1,0:T(8,128)(2,1)S(1)} async-done(((bf16[8,8,4096]{2,1,0:T(8,128)(2,1)}), bf16[8,8,4096]{2,1,0:T(8,128)(2,1)S(1)}, u32[]{:S(2)}, u32[]{:S(2)}) %all-to-all-start) | async-done | bytes 524320 | tf_op jit(solution)/shard_map/all_to_all | solution.py:267
  76.0 0.1 convert_reduce_fusion
  76.0 0.7 copy.27
  (7 shorter events, 0.1 us)
Async XLA Ops:
  0.6 0.9 %copy-start = (s32[2048]{0:T(1024)S(1)}, s32[2048]{0:T(1024)}, u32[]{:S(2)}) copy-start(s32[2048]{0:T(1024)} %param.7) | copy-start | bytes 24580
  0.6 2.1 %copy-start.3 = (s32[8]{0:T(128)S(1)}, s32[8]{0:T(128)}, u32[]{:S(2)}) copy-start(s32[8]{0:T(128)} %param.9) | copy-start | bytes 100
  0.7 2.2 %copy-start.2 = (bf16[8,32,128]{2,1,0:T(8,128)(2,1)S(1)}, bf16[8,32,128]{2,1,0:T(8,128)(2,1)}, u32[]{:S(2)}) copy-start(bf16[8,32,128]{2,1,0:T(8,128)(2,1)} %q_ref.1) | copy-start | bytes 196612
  20.5 3.4 %copy-start.1 = (bf16[256,128,128]{2,1,0:T(8,128)(2,1)S(1)}, bf16[256,128,128]{2,1,0:T(8,128)(2,1)}, u32[]{:S(2)}) copy-start(bf16[256,128,128]{2,1,0:T(8,128)(2,1)} %passages_ref.1) | copy-start | bytes 25165828
  59.5 16.4 %all-to-all-start = ((bf16[8,8,4096]{2,1,0:T(8,128)(2,1)}), bf16[8,8,4096]{2,1,0:T(8,128)(2,1)S(1)}, u32[]{:S(2)}, u32[]{:S(2)}) async-start(bf16[8,8,4096]{2,1,0:T(8,128)(2,1)} %fusion), calls=%async_computation | async-start | bytes 1048576 | tf_op jit(solution)/shard_map/all_to_all | solution.py:267
